TPU v7x, 32 devices: a whole 2x2x4 slice. The times are simulated.
32 devices in a mesh: groups: 2 (over y), dp: 4 (over x, core), owner: 4 (over z).
Axes of the slice: x: 2, y: 2, z: 4, core: 2. Of those that a mesh axis runs over, the one named last changes fastest.
Arguments:
- hidden_act: bfloat16 [4096, 28672], P(('groups', 'dp'), 'owner'), parts along dimension 0, may hold values from -6 to 6
- out_grad: bfloat16 [4096, 8192], P(('groups', 'dp'), 'owner'), parts along dimension 0, may hold values from -6 to 6
- query_left: bfloat16 [32, 8, 8192], P('dp', None, 'owner'), may hold values from -0.0078125 to 0.0078125
- query_right: bfloat16 [32, 8, 28672], P('dp', None, 'owner'), may hold values from -0.00390625 to 0.00390625
- panel_live: int32 [8, 4], P(('groups', 'dp')), parts along dimension 0, may hold values from 1 to 128, as said below
- panel_example: int32 [8, 4], P(('groups', 'dp')), parts along dimension 0, may hold values from 0 to 1, never falling along the last dimension, each value on 1 to 3 neighbouring positions
Outputs:
- scores: float32 [16, 32], P(('groups', 'dp')), parts along dimension 0
There are 2 independent parts, one for each index of `groups`. A program takes and returns all parts, laid end to end along the dimension named above; an argument that names none is the same for every part. Nothing has to cross between parts.
Inputs may be any that keep to these rules, and one draw needn't show every extreme that they name: `panel_live`: the first panel of every batch is full; every other panel holds its live tokens at its start. `panel_example`: never falls along a batch's panels; every id of 0 to 1 appears in every batch.
All inputs are finite; a program needn't handle non-finite values.
Results may differ from a plain program's by a relative error of at most 0.0003.
Values may be sent and summed in bfloat16 or wider, within the bound.
A program may use at most 64 MiB of HBM per device.

v0:
```python
import jax
import jax.numpy as jnp
from jax import lax
from jax.sharding import PartitionSpec as P

PANEL = 128
EX_DEV = 2


def shards(hidden_act, out_grad, query_left, query_right, panel_live, panel_example):
    tokens_here = hidden_act.shape[0]
    block, ranks, feat_here = query_left.shape
    dp_count = lax.axis_size("dp")
    span = 2 * ranks
    left = lax.all_gather(query_left, "dp", axis=0, tiled=True)
    count = left.shape[0]
    left_part = jnp.einsum("td,qrd->tqr", out_grad, left, preferred_element_type=jnp.float32)
    right_part = jnp.einsum(
        "tf,qrf->tqr",
        hidden_act,
        lax.all_gather(query_right, "dp", axis=0, tiled=True),
        preferred_element_type=jnp.float32,
    )
    projected = jnp.stack([left_part, right_part], axis=2).reshape(tokens_here, count * span)
    shared = lax.psum_scatter(projected, "owner", scatter_dimension=0, tiled=True)
    rows = shared.shape[0]
    paired = shared.reshape(rows, block * dp_count, 2, ranks)
    token_score = jnp.sum(paired[:, :, 0, :] * paired[:, :, 1, :], axis=2)
    position = jnp.arange(PANEL, dtype=jnp.int32)
    alive = (position[None, :] < panel_live[0][:, None]).astype(jnp.float32)
    labels = jnp.arange(EX_DEV, dtype=jnp.int32)
    onehot = (panel_example[0][:, None] == labels[None, :]).astype(jnp.float32)
    weight = (alive[:, :, None] * onehot[:, None, :]).reshape(tokens_here, EX_DEV)
    first_row = lax.axis_index("owner") * rows
    weight_rows = lax.dynamic_slice_in_dim(weight, first_row, rows, 0)
    partial_scores = jnp.dot(
        weight_rows.T,
        token_score,
        precision=lax.Precision.HIGHEST,
        preferred_element_type=jnp.float32,
    )
    return lax.psum(partial_scores, "owner")


def solution(mesh):
    return jax.shard_map(
        shards,
        mesh=mesh,
        in_specs=(
            P(("groups", "dp"), "owner"),
            P(("groups", "dp"), "owner"),
            P("dp", None, "owner"),
            P("dp", None, "owner"),
            P(("groups", "dp"), None),
            P(("groups", "dp"), None),
        ),
        out_specs=P(("groups", "dp"), None),
        check_vma=False,
    )
```

profile of v0, /device:TPU:0, one launch (start us, length us, event | category | flops | bytes accessed | tf_op | source)
XLA Modules:
  0.0 114.6 jit_solution(9959216800712294250)
XLA Ops:
  6.5 0.0 copy-start
  6.5 0.0 all-gather.3.cloned.1.call-start
  6.5 2.0 %copy.12 = bf16[8,8,2048]{2,0,1:T(8,128)(2,1)} copy(bf16[8,8,2048]{2,1,0:T(8,128)(2,1)} %param.8) | data formatting | bytes 524288 | tf_op args[2]
  8.5 0.0 all-gather.3.cloned.1.call-update
  8.5 0.0 all-gather.5.cloned.1.call-start
  8.6 2.6 %copy.13 = bf16[8,8,7168]{2,0,1:T(8,128)(2,1)} copy(bf16[8,8,7168]{2,1,0:T(8,128)(2,1)} %param.9) | data formatting | bytes 1835008 | tf_op args[3]
  11.2 0.0 all-gather.5.cloned.1.call-update
  11.2 0.0 reduce-scatter.2.cloned.1.call-start
  11.3 17.1 %all-gather.3.cloned.1.call-done = bf16[32,8,2048]{2,0,1:T(8,128)(2,1)} async-done(((bf16[8,8,2048]{2,0,1:T(8,128)(2,1)}), bf16[32,8,2048]{2,0,1:T(8,128)(2,1)}) %all-gather.3.cloned.1.call-update) | async-done | bytes 1048592 | tf_op jit(solution)/shard_map/all_gather | solution.py:15
  28.4 2.0 %fusion.4 = f32[512,32,1,8]{0,1,3,2:T(8,128)S(1)} fusion(bf16[32,8,2048]{2,0,1:T(8,128)(2,1)} %all-gather.3.cloned.1.call-done, bf16[512,2048]{1,0:T(8,128)(2,1)S(1)} %copy-done), kind=kOutput, calls=%fused_computation.4 | convolution fusion | flops 536870912 | bytes 3670016 | tf_op jit(solution)/shard_map/td,qrd->tqr/dot_general | solution.py:17
  30.4 31.1 %all-gather.5.cloned.1.call-done = bf16[32,8,7168]{2,0,1:T(8,128)(2,1)} async-done(((bf16[8,8,7168]{2,0,1:T(8,128)(2,1)}), bf16[32,8,7168]{2,0,1:T(8,128)(2,1)}) %all-gather.5.cloned.1.call-update) | async-done | bytes 3670032 | tf_op jit(solution)/shard_map/all_gather | solution.py:21
  61.5 6.2 %fusion.7 = f32[512,32,1,8]{0,1,3,2:T(8,128)S(1)} fusion(bf16[32,8,7168]{2,0,1:T(8,128)(2,1)} %all-gather.5.cloned.1.call-done, bf16[512,7168]{1,0:T(8,128)(2,1)} %param.6), kind=kOutput, calls=%fused_computation.5 | convolution fusion | flops 1879048192 | bytes 11534336 | tf_op jit(solution)/shard_map/tf,qrf->tqr/dot_general | solution.py:18
  67.7 0.0 copy-start.1
  67.7 0.0 copy-start.2
  67.7 0.1 pad_maximum_fusion
  67.8 1.6 %copy.14 = f32[512,32,2,8]{0,3,2,1:T(8,128)} copy(f32[512,32,2,8]{0,1,3,2:T(8,128)S(1)} %pad_maximum_fusion) | data formatting | bytes 2097152 | tf_op jit(solution)/shard_map/stack | solution.py:24
  69.4 0.0 reduce-scatter.2.cloned.1.call-update
  69.4 0.1 convert_bitcast_fusion
  69.5 0.1 dynamic-slice
  69.6 0.1 fusion.13
  69.7 27.1 %reduce-scatter.2.cloned.1.call-done = f32[128,512]{0,1:T(8,128)} async-done(((f32[512,512]{0,1:T(8,128)}), f32[128,512]{0,1:T(8,128)}) %reduce-scatter.2.cloned.1.call-update) | async-done | bytes 262160 | tf_op jit(solution)/shard_map/reduce_scatter | solution.py:25
  96.7 1.0 fusion.10
  97.8 0.3 fusion.11
  98.0 10.0 %psum.7 = f32[2,32]{1,0:T(2,128)} all-reduce(f32[2,32]{1,0:T(2,128)S(1)} %fusion.11), channel_id=1, replica_groups=mesh['groups'=2,'dp'=4,'owner'=4] {'owner'}, use_global_device_ids=true, to_apply=%region_2.0 | all-reduce | flops 64 | bytes 512 | tf_op jit(solution)/shard_map/psum | solution.py:42
  (4 shorter events, 0.0 us)
Async XLA Ops:
  6.5 21.8 %copy-start = (bf16[512,2048]{1,0:T(8,128)(2,1)S(1)}, bf16[512,2048]{1,0:T(8,128)(2,1)}, u32[]{:S(2)}) copy-start(bf16[512,2048]{1,0:T(8,128)(2,1)} %param.7) | copy-start | bytes 6291460
  6.5 21.8 %all-gather.3.cloned.1.call-start = ((), (), s32[]{:S(2)}) async-start(), calls=%async_computation.1 | async-start | bytes 1310720 | tf_op jit(solution)/shard_map/all_gather | solution.py:15
  8.5 53.0 %all-gather.5.cloned.1.call-start = ((), (), s32[]{:S(2)}) async-start(), calls=%async_computation.2 | async-start | bytes 4587520 | tf_op jit(solution)/shard_map/all_gather | solution.py:21
  11.2 85.5 %reduce-scatter.2.cloned.1.call-start = ((), (), s32[]{:S(2)}) async-start(), calls=%async_computation.3 | async-start | bytes 1310720 | tf_op jit(solution)/shard_map/reduce_scatter | solution.py:25
  67.7 1.7 %copy-start.1 = (s32[1,4]{1,0:T(1,128)S(1)}, s32[1,4]{1,0:T(1,128)}, u32[]{:S(2)}) copy-start(s32[1,4]{1,0:T(1,128)} %param.10) | copy-start | bytes 52
  67.7 1.9 %copy-start.2 = (s32[1,4]{1,0:T(1,128)S(1)}, s32[1,4]{1,0:T(1,128)}, u32[]{:S(2)}) copy-start(s32[1,4]{1,0:T(1,128)} %param.11) | copy-start | bytes 52
Sparse Core Ops, SparseCore 0:
  8.9 19.4 all-gather.2
  29.9 31.4 all-gather.4
  69.5 27.1 reduce-scatter.1
where the time goes:
time: 115 us
  waiting for transfers between devices  75.3 us (65%)
  between operations  13.2 us (11%)
  blocking collectives  9.98 us (9%)
  matrix products  8.45 us (7%)
  local copies, waits for them, and re-layouts  6.3 us (5%)
  other arithmetic  1.25 us (1%)
    all_gather x1, waiting for transfers between devices, shards(): lax.all_gather(query_right, 'dp', axis=0, tiled=True)  31.1 us
    reduce_scatter x1, waiting for transfers between devices, shards(): lax.psum_scatter(projected, 'owner', scatter_dimension=0, tiled=True)  27.1 us
    all_gather x1, waiting for transfers between devices, shards(): left = lax.all_gather(query_left, 'dp', axis=0, tiled=True)  17.1 us
    psum x1, blocking collectives, shards(): return lax.psum(partial_scores, 'owner')  9.98 us
    dot_general x1, matrix products, shards(): jnp.einsum('tf,qrf->tqr', hidden_act, lax.all_gather(query_right, 'dp', a...  6.21 us
    unnamed x8, local copies, waits for them, and re-layouts  4.62 us
  transfers between devices with their start and end apart: 3, of which 3 were waited for; matrix products, arithmetic and copies ran while one was open for 4% of the time, Pallas kernels for 0%

commit v1 on v0

v1 whole, which is shorter than its diff:
```python
import functools

import jax
import jax.numpy as jnp
from jax import lax
from jax.experimental import pallas as pl
from jax.experimental.pallas import tpu as pltpu
from jax.sharding import PartitionSpec as P

PANEL = 128
EX_DEV = 2
SUB = 16
F32 = jnp.float32


def remote(src, dst, send_sem, recv_sem, device):
    return pltpu.make_async_remote_copy(
        src_ref=src,
        dst_ref=dst,
        send_sem=send_sem,
        recv_sem=recv_sem,
        device_id=device,
        device_id_type=pl.DeviceIdType.MESH,
    )


def matmul_nt(a, b):
    return lax.dot_general(a, b, (((1,), (1,)), ((), ())), preferred_element_type=F32)


def kernel(
    dims,
    act_hbm,
    grad_hbm,
    ql_hbm,
    qr_hbm,
    live_ref,
    example_ref,
    out_ref,
    act,
    grad,
    ql,
    qr,
    first,
    first_in,
    unit,
    unit_in,
    sums,
    ends,
    load_sem,
    own_sem,
    sib_send,
    sib_recv,
    x_send,
    x_recv,
    xs_send,
    xs_recv,
    y_send,
    y_recv,
    ys_send,
    ys_recv,
    z_send,
    z_recv,
    end_send,
    end_recv,
):
    chips, owners, splits = dims
    pieces = splits + 1
    tokens = act.shape[0]
    panels = tokens // PANEL
    half = panels // 2
    width = act.shape[1] // splits
    g = lax.axis_index("groups")
    d = lax.axis_index("dp")
    o = lax.axis_index("owner")
    x = d // 2
    core = d % 2
    sibling = {"dp": 2 * x + 1 - core}
    across = {"groups": 1 - g}

    def columns(f):
        return pl.ds((f - 1) * width, width)

    def block(s, h, a, f):
        return ql.at[s, h, a] if f == 0 else qr.at[s, h, a, :, columns(f)]

    def whole_block(s, f):
        return ql.at[s] if f == 0 else qr.at[s, :, :, :, columns(f)]

    own_loads = [
        pltpu.make_async_copy(ql_hbm, ql.at[d], own_sem.at[0]),
        pltpu.make_async_copy(qr_hbm, qr.at[d], own_sem.at[1]),
    ]
    for copy in own_loads:
        copy.start()
    loads = [pltpu.make_async_copy(grad_hbm, grad, load_sem.at[0])]
    for f in range(1, pieces):
        loads.append(
            pltpu.make_async_copy(act_hbm.at[:, columns(f)], act.at[:, columns(f)], load_sem.at[f])
        )
    for copy in loads:
        copy.start()

    barrier = pltpu.get_barrier_semaphore()
    peers = [sibling, across]
    peers += [{"dp": 2 * lax.rem(x + k, chips) + core} for k in range(1, chips)]
    peers += [{"owner": lax.rem(o + k, owners)} for k in range(1, owners)]
    for peer in peers:
        pl.semaphore_signal(barrier, inc=1, device_id=peer, device_id_type=pl.DeviceIdType.MESH)
    sums[...] = jnp.zeros_like(sums)
    for copy in own_loads:
        copy.wait()
    pl.semaphore_wait(barrier, len(peers))

    sends = []

    def send(src, dst, send_sem, recv_sem, device):
        copy = remote(src, dst, send_sem, recv_sem, device)
        copy.start()
        sends.append(copy)

    def arrived(ref, send_sem, recv_sem, device):
        remote(ref, ref, send_sem, recv_sem, device).wait_recv()

    order = [(k, a, f) for k in range(1, chips) for a in range(2) for f in range(pieces)]
    count = len(order)
    for f in range(pieces):
        if f < count:
            k, a, p = order[f]
            ref = block(d, g, a, p)
            send(ref, ref, x_send.at[f], x_recv.at[f], {"dp": 2 * lax.rem(x + k, chips) + core})
        ref = whole_block(d, f)
        send(ref, ref, sib_send.at[f], sib_recv.at[f], sibling)
    for i in range(pieces, count):
        k, a, p = order[i]
        ref = block(d, g, a, p)
        send(ref, ref, x_send.at[i], x_recv.at[i], {"dp": 2 * lax.rem(x + k, chips) + core})

    def chip_of(k):
        return lax.rem(x + chips - k, chips)

    def partial(u):
        return (first, first_in) if u == 0 else (unit.at[u - 1], unit_in.at[u - 1])

    def line_step(u, j, up):
        total, incoming = partial(u)
        lanes = total.shape[1]
        target = {"owner": lax.rem(o + 1, owners) if up else lax.rem(o + owners - 1, owners)}
        for sub in range(half):
            p = half + sub if up else sub
            rows = pl.ds(p * PANEL, PANEL)
            slot = u * panels + p
            if j > 0:
                arrived(incoming.at[rows], z_send.at[slot], z_recv.at[slot], target)
            if 0 < j < owners - 1:
                total[rows, :] = total[rows, :] + incoming[rows, :]
            if j < owners - 1:
                remote(
                    total.at[rows], incoming.at[rows], z_send.at[slot], z_recv.at[slot], target
                ).start()
            else:
                value = total[rows, :] + incoming[rows, :]
                if lanes == 256:
                    product = value[:, :128] * value[:, 128:]
                else:
                    product = value * pltpu.roll(value, 64, 1)
                position = lax.broadcasted_iota(jnp.int32, (PANEL, 128), 0)
                kept = jnp.where(position < live_ref[0, p], product, 0.0)
                row = jnp.sum(kept, axis=0, keepdims=True)
                label = lax.broadcasted_iota(jnp.int32, (8, 128), 0)
                sums[u] = sums[u] + jnp.where(label == example_ref[0, p], row, 0.0)

    def line(u, j):
        @pl.when(o == owners - 1 - j)
        def _():
            line_step(u, j, False)

        @pl.when(o == j)
        def _():
            line_step(u, j, True)

    units = 1 + 2 * (chips - 1)
    events = {}
    for u in range(units):
        ready = pieces - 1 if u == 0 else pieces * u + 1
        last = u == units - 1
        for j in range(owners):
            at = ready + (j if last else 2 * j)
            events.setdefault(at, []).append((u, j))

    for i in range(max(events) + 1):
        if i < count:
            k, a, f = order[i]
            ref = block(2 * chip_of(k) + core, g, a, f)
            arrived(ref, x_send.at[i], x_recv.at[i], sibling)
            send(ref, ref, y_send.at[i], y_recv.at[i], across)
            send(ref, ref, xs_send.at[i], xs_recv.at[i], sibling)
        if 1 <= i <= count:
            k, a, f = order[i - 1]
            ref = block(2 * chip_of(k) + core, 1 - g, a, f)
            arrived(ref, y_send.at[i - 1], y_recv.at[i - 1], across)
            send(ref, ref, ys_send.at[i - 1], ys_recv.at[i - 1], sibling)
        if i < pieces:
            loads[i].wait()
            arrived(
                whole_block(2 * x + 1 - core, i), sib_send.at[i], sib_recv.at[i], sibling
            )
            if i == 0:
                rhs = ql[pl.ds(2 * x, 2)].reshape(128, ql.shape[-1])
                first[:, :128] = matmul_nt(grad[...], rhs)
            else:
                cols = columns(i)
                rhs = qr[pl.ds(2 * x, 2), :, :, :, cols].reshape(128, width)
                part = matmul_nt(act[:, cols], rhs)
                first[:, 128:] = part if i == 1 else first[:, 128:] + part
        if 2 <= i < count + 2:
            k, a, f = order[i - 2]
            source = chip_of(k)
            other = 2 * source + 1 - core
            arrived(block(other, g, a, f), xs_send.at[i - 2], xs_recv.at[i - 2], sibling)
            arrived(block(other, 1 - g, a, f), ys_send.at[i - 2], ys_recv.at[i - 2], sibling)
            u = 2 * (k - 1) + a
            if f == 0:
                rhs = ql[pl.ds(2 * source, 2), :, a].reshape(64, ql.shape[-1])
                rhs = jnp.concatenate([rhs, jnp.zeros_like(rhs)], axis=0)
                unit[u] = matmul_nt(grad[...], rhs)
            else:
                cols = columns(f)
                rhs = qr[pl.ds(2 * source, 2), :, a, :, cols].reshape(64, width)
                rhs = jnp.concatenate([jnp.zeros_like(rhs), rhs], axis=0)
                unit[u] = unit[u] + matmul_nt(act[:, cols], rhs)
        for u, j in events.get(i, ()):
            line(u, j)

    def end_copies(e):
        return [
            remote(
                ends.at[e],
                ends.at[e],
                end_send.at[e, k],
                end_recv.at[e],
                {"owner": lax.rem(o + k, owners)},
            )
            for k in range(1, owners)
        ]

    lane = lax.broadcasted_iota(jnp.int32, (128, ends.shape[-1]), 0)
    query = lax.broadcasted_iota(jnp.int32, (128, ends.shape[-1]), 1)
    for e in range(2):

        @pl.when(o == (owners - 1) * e)
        def _(e=e):
            spread = (query == 16 * x + lane // 8).astype(F32)
            result = jnp.dot(
                sums[0], spread, precision=lax.Precision.HIGHEST, preferred_element_type=F32
            )
            for k in range(1, chips):
                for a in range(2):
                    u = 1 + 2 * (k - 1) + a
                    place = (lane // 32) * 8 + (lane % 32) // 16 * 4 + 2 * a + (lane % 16) // 8
                    hit = (query == 16 * chip_of(k) + place) & (lane < 64)
                    result = result + jnp.dot(
                        sums[u],
                        hit.astype(F32),
                        precision=lax.Precision.HIGHEST,
                        preferred_element_type=F32,
                    )
            ends[e] = result
            for copy in end_copies(e):
                copy.start()

    for e in range(2):

        @pl.when(o != (owners - 1) * e)
        def _(e=e):
            arrived(ends.at[e], end_send.at[e, 1], end_recv.at[e], sibling)

    both = ends[0] + ends[1]
    out_ref[...] = both[: out_ref.shape[0], : out_ref.shape[1]]

    for copy in sends:
        copy.wait_send()
    for u in range(units):
        total, incoming = partial(u)
        for p in range(panels):
            rows = pl.ds(p * PANEL, PANEL)
            slot = u * panels + p

            @pl.when(o < owners - 1 if p >= half else o > 0)
            def _(total=total, incoming=incoming, rows=rows, slot=slot):
                remote(
                    total.at[rows], incoming.at[rows], z_send.at[slot], z_recv.at[slot], sibling
                ).wait_send()

    for e in range(2):

        @pl.when(o == (owners - 1) * e)
        def _(e=e):
            for copy in end_copies(e):
                copy.wait_send()


def shards(sizes, hidden_act, out_grad, query_left, query_right, panel_live, panel_example):
    chips, owners = sizes
    tokens, units_here = hidden_act.shape
    feat_here = out_grad.shape[1]
    block, ranks, _ = query_left.shape
    splits = 4 if chips == 2 else 1
    pieces = splits + 1
    count = 2 * (chips - 1) * pieces
    units = 1 + 2 * (chips - 1)
    queries = block * 2 * chips
    wide = -(-queries // 128) * 128
    panels = tokens // PANEL
    ql = query_left.reshape(2, 2, SUB, feat_here)
    qr = query_right.reshape(2, 2, SUB, units_here)
    dma = pltpu.SemaphoreType.DMA
    anywhere = pl.BlockSpec(memory_space=pl.ANY)
    smem = pl.BlockSpec(memory_space=pltpu.SMEM)
    return pl.pallas_call(
        functools.partial(kernel, (chips, owners, splits)),
        out_shape=jax.ShapeDtypeStruct((EX_DEV, queries), F32),
        in_specs=[anywhere] * 4 + [smem] * 2,
        out_specs=pl.BlockSpec(memory_space=pltpu.VMEM),
        scratch_shapes=[
            pltpu.VMEM((tokens, units_here), jnp.bfloat16),
            pltpu.VMEM((tokens, feat_here), jnp.bfloat16),
            pltpu.VMEM((2 * chips, 2, 2, SUB, feat_here), jnp.bfloat16),
            pltpu.VMEM((2 * chips, 2, 2, SUB, units_here), jnp.bfloat16),
            pltpu.VMEM((tokens, 256), F32),
            pltpu.VMEM((tokens, 256), F32),
            pltpu.VMEM((units - 1, tokens, 128), F32),
            pltpu.VMEM((units - 1, tokens, 128), F32),
            pltpu.VMEM((units, 8, 128), F32),
            pltpu.VMEM((2, 8, wide), F32),
            dma((pieces,)),
            dma((2,)),
            dma((pieces,)),
            dma((pieces,)),
        ]
        + [dma((count,))] * 8
        + [
            dma((units * panels,)),
            dma((units * panels,)),
            dma((2, owners)),
            dma((2,)),
        ],
        compiler_params=pltpu.CompilerParams(
            collective_id=0, has_side_effects=True, vmem_limit_bytes=56 * 1024 * 1024
        ),
    )(hidden_act, out_grad, ql, qr, panel_live, panel_example)


def solution(mesh):
    sizes = (mesh.shape["dp"] // 2, mesh.shape["owner"])
    return jax.shard_map(
        functools.partial(shards, sizes),
        mesh=mesh,
        in_specs=(
            P(("groups", "dp"), "owner"),
            P(("groups", "dp"), "owner"),
            P("dp", None, "owner"),
            P("dp", None, "owner"),
            P(("groups", "dp"), None),
            P(("groups", "dp"), None),
        ),
        out_specs=P(("groups", "dp"), None),
        check_vma=False,
    )
```

time: 115 us -> 59.7 us (0.52)
  waiting for transfers between devices: 75.3 us -> 0 us
  Pallas kernels: 0 us -> 58.3 us
  between operations: 13.2 us -> 0.01 us
  blocking collectives: 9.98 us -> 0 us
  matrix products: 8.45 us -> 0 us
  local copies, waits for them, and re-layouts: 6.3 us -> 1.24 us
  other arithmetic: 1.25 us -> 0 us
    pallas_call x0 -> x1, Pallas kernels: none -> 58.3 us  [shards(): pl.pallas_call(functools.partial(kernel, (chips, owners, splits)), out_sh...]
    all_gather x2 -> x0, waiting for transfers between devices: 48.2 us -> none  [the longest x1 31.1 us: shards(): lax.all_gather(query_right, 'dp', axis=0, tiled=True)]
    reduce_scatter x1 -> x0, waiting for transfers between devices: 27.1 us -> none  [shards(): lax.psum_scatter(projected, 'owner', scatter_dimension=0, tiled=True)]
    psum x1 -> x0, blocking collectives: 9.98 us -> none  [shards(): return lax.psum(partial_scores, 'owner')]
    dot_general x3 -> x0, matrix products: 8.45 us -> none  [the longest x1 6.21 us: shards(): jnp.einsum('tf,qrf->tqr', hidden_act, lax.all_gather(query_right, 'dp', a...]
    unnamed x8 -> x1, local copies, waits for them, and re-layouts: 4.62 us -> 1.24 us
    another operation x1 -> x0, local copies, waits for them, and re-layouts: 1.58 us -> none  [shards(): jnp.stack([left_part, right_part], axis=2)]
  transfers between devices with their start and end apart: 3 -> 0, of which waited for: 3 -> 0; matrix products, arithmetic and copies ran while one was open for 4% -> 0% of each run, Pallas kernels for 0% -> 0%
where the time goes in v1:
time: 59.7 us; the launch traced here: 59.6 us
  Pallas kernels  58.3 us (98%)
  local copies, waits for them, and re-layouts  1.24 us (2%)
    pallas_call x1, Pallas kernels, shards(): pl.pallas_call(functools.partial(kernel, (chips, owners, splits)), out_sh...  58.3 us
    unnamed x1, local copies, waits for them, and re-layouts  1.24 us

profile of v1, /device:TPU:0, one launch (start us, length us, event | category | flops | bytes accessed | tf_op | source)
XLA Modules:
  0.0 59.6 jit_solution(562047886733544091)
XLA Ops:
  0.0 58.3 %shard_map.64 = f32[2,32]{1,0:T(2,128)} custom-call(bf16[512,7168]{1,0:T(8,128)(2,1)} %act_hbm.1, bf16[512,2048]{1,0:T(8,128)(2,1)} %grad_hbm.1, bf16[2,2,16,2048]{3,2,1,0:T(8,128)(2,1)} %bitcast.3, bf16[2,2,16,7168]{3,2,1,0:T(8,128)(2,1)} %bitcast.2, s32[1,4]{1,0:T(1,128)} %live_ref.1, s32[1,4]{1,0:T(1,128)} %example_ref.1), custom_call_target="tpu_custom_call" | custom-call | tf_op jit(solution)/shard_map/pallas_call | solution.py:320
  58.3 1.2 %copy.8 = f32[2,32]{1,0:T(2,128)} copy(f32[2,32]{1,0:T(2,128)} %shard_map.64) | data formatting | bytes 512

commit v2 on v1

--- a/solution.py
+++ b/solution.py
@@ -10,6 +10,8 @@
 PANEL = 128
 EX_DEV = 2
 SUB = 16
+LOOK = 2
+EARLY = 2
 F32 = jnp.float32
 
 
@@ -67,8 +69,7 @@
     chips, owners, splits = dims
     pieces = splits + 1
     tokens = act.shape[0]
-    panels = tokens // PANEL
-    half = panels // 2
+    share = tokens // owners
     width = act.shape[1] // splits
     g = lax.axis_index("groups")
     d = lax.axis_index("dp")
@@ -98,7 +99,7 @@
         loads.append(
             pltpu.make_async_copy(act_hbm.at[:, columns(f)], act.at[:, columns(f)], load_sem.at[f])
         )
-    for copy in loads:
+    for copy in loads[:EARLY]:
         copy.start()
 
     barrier = pltpu.get_barrier_semaphore()
@@ -124,17 +125,20 @@
 
     order = [(k, a, f) for k in range(1, chips) for a in range(2) for f in range(pieces)]
     count = len(order)
+
+    def send_across_x(i):
+        if i < count:
+            k, a, p = order[i]
+            ref = block(d, g, a, p)
+            send(ref, ref, x_send.at[i], x_recv.at[i], {"dp": 2 * lax.rem(x + k, chips) + core})
+
+    for i in range(LOOK):
+        send_across_x(i)
     for f in range(pieces):
-        if f < count:
-            k, a, p = order[f]
-            ref = block(d, g, a, p)
-            send(ref, ref, x_send.at[f], x_recv.at[f], {"dp": 2 * lax.rem(x + k, chips) + core})
         ref = whole_block(d, f)
         send(ref, ref, sib_send.at[f], sib_recv.at[f], sibling)
-    for i in range(pieces, count):
-        k, a, p = order[i]
-        ref = block(d, g, a, p)
-        send(ref, ref, x_send.at[i], x_recv.at[i], {"dp": 2 * lax.rem(x + k, chips) + core})
+    for copy in loads[EARLY:]:
+        copy.start()
 
     def chip_of(k):
         return lax.rem(x + chips - k, chips)
@@ -142,57 +146,57 @@
     def partial(u):
         return (first, first_in) if u == 0 else (unit.at[u - 1], unit_in.at[u - 1])
 
-    def line_step(u, j, up):
+    def z_peer(k):
+        return lax.rem(o + k, owners)
+
+    def z_copy(u, k):
         total, incoming = partial(u)
-        lanes = total.shape[1]
-        target = {"owner": lax.rem(o + 1, owners) if up else lax.rem(o + owners - 1, owners)}
-        for sub in range(half):
-            p = half + sub if up else sub
-            rows = pl.ds(p * PANEL, PANEL)
-            slot = u * panels + p
-            if j > 0:
-                arrived(incoming.at[rows], z_send.at[slot], z_recv.at[slot], target)
-            if 0 < j < owners - 1:
-                total[rows, :] = total[rows, :] + incoming[rows, :]
-            if j < owners - 1:
-                remote(
-                    total.at[rows], incoming.at[rows], z_send.at[slot], z_recv.at[slot], target
-                ).start()
-            else:
-                value = total[rows, :] + incoming[rows, :]
-                if lanes == 256:
-                    product = value[:, :128] * value[:, 128:]
-                else:
-                    product = value * pltpu.roll(value, 64, 1)
-                position = lax.broadcasted_iota(jnp.int32, (PANEL, 128), 0)
-                kept = jnp.where(position < live_ref[0, p], product, 0.0)
-                row = jnp.sum(kept, axis=0, keepdims=True)
-                label = lax.broadcasted_iota(jnp.int32, (8, 128), 0)
-                sums[u] = sums[u] + jnp.where(label == example_ref[0, p], row, 0.0)
-
-    def line(u, j):
-        @pl.when(o == owners - 1 - j)
-        def _():
-            line_step(u, j, False)
-
-        @pl.when(o == j)
-        def _():
-            line_step(u, j, True)
+        slot = u * owners + k
+        rows = pl.ds(pl.multiple_of(z_peer(k) * share, share), share)
+        return remote(
+            total.at[rows],
+            incoming.at[k - 1],
+            z_send.at[slot],
+            z_recv.at[slot],
+            {"owner": z_peer(k)},
+        )
+
+    def scatter(u):
+        for k in range(1, owners):
+            z_copy(u, k).start()
+
+    def finish(u):
+        total, incoming = partial(u)
+        for k in range(1, owners):
+            z_copy(u, k).wait_recv()
+        value = total[pl.ds(pl.multiple_of(o * share, share), share), :]
+        for k in range(1, owners):
+            value = value + incoming[k - 1]
+        if value.shape[1] == 256:
+            product = value[:, :128] * value[:, 128:]
+        else:
+            product = value * pltpu.roll(value, 64, 1)
+        for start in range(0, share, min(share, PANEL)):
+            rows = min(share, PANEL)
+            token = o * share + start
+            panel = token // PANEL
+            position = lax.broadcasted_iota(jnp.int32, (rows, 128), 0) + token % PANEL
+            kept = jnp.where(position < live_ref[0, panel], product[start : start + rows], 0.0)
+            row = jnp.sum(kept, axis=0, keepdims=True)
+            label = lax.broadcasted_iota(jnp.int32, (8, 128), 0)
+            sums[u] = sums[u] + jnp.where(label == example_ref[0, panel], row, 0.0)
 
     units = 1 + 2 * (chips - 1)
-    events = {}
-    for u in range(units):
-        ready = pieces - 1 if u == 0 else pieces * u + 1
-        last = u == units - 1
-        for j in range(owners):
-            at = ready + (j if last else 2 * j)
-            events.setdefault(at, []).append((u, j))
-
-    for i in range(max(events) + 1):
+    ready = {pieces - 1: 0}
+    for u in range(1, units):
+        ready[pieces * u + 1] = u
+
+    for i in range(max(ready) + 1):
         if i < count:
             k, a, f = order[i]
             ref = block(2 * chip_of(k) + core, g, a, f)
             arrived(ref, x_send.at[i], x_recv.at[i], sibling)
+            send_across_x(i + LOOK)
             send(ref, ref, y_send.at[i], y_recv.at[i], across)
             send(ref, ref, xs_send.at[i], xs_recv.at[i], sibling)
         if 1 <= i <= count:
@@ -229,75 +233,52 @@
                 rhs = qr[pl.ds(2 * source, 2), :, a, :, cols].reshape(64, width)
                 rhs = jnp.concatenate([jnp.zeros_like(rhs), rhs], axis=0)
                 unit[u] = unit[u] + matmul_nt(act[:, cols], rhs)
-        for u, j in events.get(i, ()):
-            line(u, j)
-
-    def end_copies(e):
-        return [
-            remote(
-                ends.at[e],
-                ends.at[e],
-                end_send.at[e, k],
-                end_recv.at[e],
-                {"owner": lax.rem(o + k, owners)},
-            )
-            for k in range(1, owners)
-        ]
+        if i in ready:
+            scatter(ready[i])
+
+    for u in range(units):
+        finish(u)
 
     lane = lax.broadcasted_iota(jnp.int32, (128, ends.shape[-1]), 0)
     query = lax.broadcasted_iota(jnp.int32, (128, ends.shape[-1]), 1)
-    for e in range(2):
-
-        @pl.when(o == (owners - 1) * e)
-        def _(e=e):
-            spread = (query == 16 * x + lane // 8).astype(F32)
-            result = jnp.dot(
-                sums[0], spread, precision=lax.Precision.HIGHEST, preferred_element_type=F32
+    spread = (query == 16 * x + lane // 8).astype(F32)
+    result = jnp.dot(
+        sums[0], spread, precision=lax.Precision.HIGHEST, preferred_element_type=F32
+    )
+    for k in range(1, chips):
+        for a in range(2):
+            u = 1 + 2 * (k - 1) + a
+            place = (lane // 32) * 8 + (lane % 32) // 16 * 4 + 2 * a + (lane % 16) // 8
+            hit = (query == 16 * chip_of(k) + place) & (lane < 64)
+            result = result + jnp.dot(
+                sums[u],
+                hit.astype(F32),
+                precision=lax.Precision.HIGHEST,
+                preferred_element_type=F32,
             )
-            for k in range(1, chips):
-                for a in range(2):
-                    u = 1 + 2 * (k - 1) + a
-                    place = (lane // 32) * 8 + (lane % 32) // 16 * 4 + 2 * a + (lane % 16) // 8
-                    hit = (query == 16 * chip_of(k) + place) & (lane < 64)
-                    result = result + jnp.dot(
-                        sums[u],
-                        hit.astype(F32),
-                        precision=lax.Precision.HIGHEST,
-                        preferred_element_type=F32,
-                    )
-            ends[e] = result
-            for copy in end_copies(e):
-                copy.start()
-
-    for e in range(2):
-
-        @pl.when(o != (owners - 1) * e)
-        def _(e=e):
-            arrived(ends.at[e], end_send.at[e, 1], end_recv.at[e], sibling)
-
-    both = ends[0] + ends[1]
+    ends[o] = result
+    end_copies = [
+        remote(
+            ends.at[o], ends.at[o], end_send.at[k], end_recv.at[k], {"owner": z_peer(k)}
+        )
+        for k in range(1, owners)
+    ]
+    for copy in end_copies:
+        copy.start()
+    for k in range(1, owners):
+        arrived(ends.at[z_peer(owners - k)], end_send.at[k], end_recv.at[k], sibling)
+    both = ends[0]
+    for e in range(1, owners):
+        both = both + ends[e]
     out_ref[...] = both[: out_ref.shape[0], : out_ref.shape[1]]
 
     for copy in sends:
         copy.wait_send()
     for u in range(units):
-        total, incoming = partial(u)
-        for p in range(panels):
-            rows = pl.ds(p * PANEL, PANEL)
-            slot = u * panels + p
-
-            @pl.when(o < owners - 1 if p >= half else o > 0)
-            def _(total=total, incoming=incoming, rows=rows, slot=slot):
-                remote(
-                    total.at[rows], incoming.at[rows], z_send.at[slot], z_recv.at[slot], sibling
-                ).wait_send()
-
-    for e in range(2):
-
-        @pl.when(o == (owners - 1) * e)
-        def _(e=e):
-            for copy in end_copies(e):
-                copy.wait_send()
+        for k in range(1, owners):
+            z_copy(u, k).wait_send()
+    for copy in end_copies:
+        copy.wait_send()
 
 
 def shards(sizes, hidden_act, out_grad, query_left, query_right, panel_live, panel_example):
@@ -311,7 +292,7 @@
     units = 1 + 2 * (chips - 1)
     queries = block * 2 * chips
     wide = -(-queries // 128) * 128
-    panels = tokens // PANEL
+    share = tokens // owners
     ql = query_left.reshape(2, 2, SUB, feat_here)
     qr = query_right.reshape(2, 2, SUB, units_here)
     dma = pltpu.SemaphoreType.DMA
@@ -328,11 +309,11 @@
             pltpu.VMEM((2 * chips, 2, 2, SUB, feat_here), jnp.bfloat16),
             pltpu.VMEM((2 * chips, 2, 2, SUB, units_here), jnp.bfloat16),
             pltpu.VMEM((tokens, 256), F32),
-            pltpu.VMEM((tokens, 256), F32),
+            pltpu.VMEM((owners - 1, share, 256), F32),
             pltpu.VMEM((units - 1, tokens, 128), F32),
-            pltpu.VMEM((units - 1, tokens, 128), F32),
+            pltpu.VMEM((units - 1, owners - 1, share, 128), F32),
             pltpu.VMEM((units, 8, 128), F32),
-            pltpu.VMEM((2, 8, wide), F32),
+            pltpu.VMEM((owners, 8, wide), F32),
             dma((pieces,)),
             dma((2,)),
             dma((pieces,)),
@@ -340,10 +321,10 @@
         ]
         + [dma((count,))] * 8
         + [
-            dma((units * panels,)),
-            dma((units * panels,)),
-            dma((2, owners)),
-            dma((2,)),
+            dma((units * owners,)),
+            dma((units * owners,)),
+            dma((owners,)),
+            dma((owners,)),
         ],
         compiler_params=pltpu.CompilerParams(
             collective_id=0, has_side_effects=True, vmem_limit_bytes=56 * 1024 * 1024

time: 59.7 us -> 51.3 us (0.86)
  Pallas kernels: 58.3 us -> 49.9 us
    pallas_call x1, Pallas kernels: 58.3 us -> 49.9 us  [shards(): pl.pallas_call(functools.partial(kernel, (chips, owners, splits)), out_sh...]
where the time goes in v2:
time: 51.3 us; the launch traced here: 51.1 us
  Pallas kernels  49.9 us (97%)
  local copies, waits for them, and re-layouts  1.24 us (2%)
    pallas_call x1, Pallas kernels, shards(): pl.pallas_call(functools.partial(kernel, (chips, owners, splits)), out_sh...  49.9 us
    unnamed x1, local copies, waits for them, and re-layouts  1.24 us

profile of v2, /device:TPU:0, one launch (start us, length us, event | category | flops | bytes accessed | tf_op | source)
XLA Modules:
  0.0 51.1 jit_solution(4188436145831498470)
XLA Ops:
  0.0 49.9 %shard_map.64 = f32[2,32]{1,0:T(2,128)} custom-call(bf16[512,7168]{1,0:T(8,128)(2,1)} %act_hbm.1, bf16[512,2048]{1,0:T(8,128)(2,1)} %grad_hbm.1, bf16[2,2,16,2048]{3,2,1,0:T(8,128)(2,1)} %bitcast.3, bf16[2,2,16,7168]{3,2,1,0:T(8,128)(2,1)} %bitcast.2, s32[1,4]{1,0:T(1,128)} %live_ref.1, s32[1,4]{1,0:T(1,128)} %example_ref.1), custom_call_target="tpu_custom_call" | custom-call | tf_op jit(solution)/shard_map/pallas_call | solution.py:301
  49.9 1.2 %copy.8 = f32[2,32]{1,0:T(2,128)} copy(f32[2,32]{1,0:T(2,128)} %shard_map.64) | data formatting | bytes 512

commit v3 on v2

--- a/solution.py
+++ b/solution.py
@@ -10,7 +10,9 @@
 PANEL = 128
 EX_DEV = 2
 SUB = 16
-LOOK = 2
+LOOK = 4
+Y_LAG = 3
+USE_LAG = 5
 EARLY = 2
 F32 = jnp.float32
 
@@ -189,7 +191,7 @@
     units = 1 + 2 * (chips - 1)
     ready = {pieces - 1: 0}
     for u in range(1, units):
-        ready[pieces * u + 1] = u
+        ready[pieces * u - 1 + USE_LAG] = u
 
     for i in range(max(ready) + 1):
         if i < count:
@@ -199,11 +201,11 @@
             send_across_x(i + LOOK)
             send(ref, ref, y_send.at[i], y_recv.at[i], across)
             send(ref, ref, xs_send.at[i], xs_recv.at[i], sibling)
-        if 1 <= i <= count:
-            k, a, f = order[i - 1]
+        if Y_LAG <= i < count + Y_LAG:
+            k, a, f = order[i - Y_LAG]
             ref = block(2 * chip_of(k) + core, 1 - g, a, f)
-            arrived(ref, y_send.at[i - 1], y_recv.at[i - 1], across)
-            send(ref, ref, ys_send.at[i - 1], ys_recv.at[i - 1], sibling)
+            arrived(ref, y_send.at[i - Y_LAG], y_recv.at[i - Y_LAG], across)
+            send(ref, ref, ys_send.at[i - Y_LAG], ys_recv.at[i - Y_LAG], sibling)
         if i < pieces:
             loads[i].wait()
             arrived(
@@ -217,12 +219,12 @@
                 rhs = qr[pl.ds(2 * x, 2), :, :, :, cols].reshape(128, width)
                 part = matmul_nt(act[:, cols], rhs)
                 first[:, 128:] = part if i == 1 else first[:, 128:] + part
-        if 2 <= i < count + 2:
-            k, a, f = order[i - 2]
+        if USE_LAG <= i < count + USE_LAG:
+            k, a, f = order[i - USE_LAG]
             source = chip_of(k)
             other = 2 * source + 1 - core
-            arrived(block(other, g, a, f), xs_send.at[i - 2], xs_recv.at[i - 2], sibling)
-            arrived(block(other, 1 - g, a, f), ys_send.at[i - 2], ys_recv.at[i - 2], sibling)
+            arrived(block(other, g, a, f), xs_send.at[i - USE_LAG], xs_recv.at[i - USE_LAG], sibling)
+            arrived(block(other, 1 - g, a, f), ys_send.at[i - USE_LAG], ys_recv.at[i - USE_LAG], sibling)
             u = 2 * (k - 1) + a
             if f == 0:
                 rhs = ql[pl.ds(2 * source, 2), :, a].reshape(64, ql.shape[-1])

time: 51.3 us -> 45.5 us (0.89)
  Pallas kernels: 49.9 us -> 44.1 us
    pallas_call x1, Pallas kernels: 49.9 us -> 44.1 us  [shards(): pl.pallas_call(functools.partial(kernel, (chips, owners, splits)), out_sh...]
where the time goes in v3:
time: 45.5 us; the launch traced here: 45.3 us
  Pallas kernels  44.1 us (97%)
  local copies, waits for them, and re-layouts  1.24 us (3%)
    pallas_call x1, Pallas kernels, shards(): pl.pallas_call(functools.partial(kernel, (chips, owners, splits)), out_sh...  44.1 us
    unnamed x1, local copies, waits for them, and re-layouts  1.24 us

profile of v3, /device:TPU:0, one launch (start us, length us, event | category | flops | bytes accessed | tf_op | source)
XLA Modules:
  0.0 45.3 jit_solution(17140703500466733277)
XLA Ops:
  0.0 44.1 %shard_map.64 = f32[2,32]{1,0:T(2,128)} custom-call(bf16[512,7168]{1,0:T(8,128)(2,1)} %act_hbm.1, bf16[512,2048]{1,0:T(8,128)(2,1)} %grad_hbm.1, bf16[2,2,16,2048]{3,2,1,0:T(8,128)(2,1)} %bitcast.3, bf16[2,2,16,7168]{3,2,1,0:T(8,128)(2,1)} %bitcast.2, s32[1,4]{1,0:T(1,128)} %live_ref.1, s32[1,4]{1,0:T(1,128)} %example_ref.1), custom_call_target="tpu_custom_call" | custom-call | tf_op jit(solution)/shard_map/pallas_call | solution.py:303
  44.1 1.2 %copy.8 = f32[2,32]{1,0:T(2,128)} copy(f32[2,32]{1,0:T(2,128)} %shard_map.64) | data formatting | bytes 512

commit v4 on v3

--- a/solution.py
+++ b/solution.py
@@ -10,7 +10,7 @@
 PANEL = 128
 EX_DEV = 2
 SUB = 16
-LOOK = 4
+LOOK = 10
 Y_LAG = 3
 USE_LAG = 5
 EARLY = 2
@@ -234,9 +234,16 @@
                 cols = columns(f)
                 rhs = qr[pl.ds(2 * source, 2), :, a, :, cols].reshape(64, width)
                 rhs = jnp.concatenate([jnp.zeros_like(rhs), rhs], axis=0)
-                unit[u] = unit[u] + matmul_nt(act[:, cols], rhs)
-        if i in ready:
-            scatter(ready[i])
+                if f < pieces - 1:
+                    unit[u] = unit[u] + matmul_nt(act[:, cols], rhs)
+                else:
+                    for step in range(1, owners + 1):
+                        rows = pl.ds(pl.multiple_of(z_peer(step) * share, share), share)
+                        unit[u, rows] = unit[u, rows] + matmul_nt(act[rows, cols], rhs)
+                        if step < owners:
+                            z_copy(u + 1, step).start()
+        if i == pieces - 1:
+            scatter(0)
 
     for u in range(units):
         finish(u)

time: 45.5 us -> 45.5 us (level)
  no operation moved by 1% of the time
where the time goes in v4:
time: 45.5 us; the launch traced here: 45.3 us
  Pallas kernels  44.1 us (97%)
  local copies, waits for them, and re-layouts  1.24 us (3%)
    pallas_call x1, Pallas kernels, shards(): pl.pallas_call(functools.partial(kernel, (chips, owners, splits)), out_sh...  44.1 us
    unnamed x1, local copies, waits for them, and re-layouts  1.24 us

profile of v4, /device:TPU:0, one launch (start us, length us, event | category | flops | bytes accessed | tf_op | source)
XLA Modules:
  0.0 45.3 jit_solution(5773114239836572761)
XLA Ops:
  0.0 44.1 %shard_map.64 = f32[2,32]{1,0:T(2,128)} custom-call(bf16[512,7168]{1,0:T(8,128)(2,1)} %act_hbm.1, bf16[512,2048]{1,0:T(8,128)(2,1)} %grad_hbm.1, bf16[2,2,16,2048]{3,2,1,0:T(8,128)(2,1)} %bitcast.3, bf16[2,2,16,7168]{3,2,1,0:T(8,128)(2,1)} %bitcast.2, s32[1,4]{1,0:T(1,128)} %live_ref.1, s32[1,4]{1,0:T(1,128)} %example_ref.1), custom_call_target="tpu_custom_call" | custom-call | tf_op jit(solution)/shard_map/pallas_call | solution.py:310
  44.1 1.2 %copy.8 = f32[2,32]{1,0:T(2,128)} copy(f32[2,32]{1,0:T(2,128)} %shard_map.64) | data formatting | bytes 512
